TPU v7x, 32 devices: a whole 2x2x4 slice. The times are simulated.
32 devices in a mesh: grp: 4 (over y, x), line: 8 (over z, core).
Axes of the slice: x: 2, y: 2, z: 4, core: 2. Of those that a mesh axis runs over, the one named last changes fastest.
Arguments:
- raw_echo: bfloat16 [2, 4096, 65536], P(None, ('grp', 'line')), may hold values from -6 to 6
- valid_lines: int32 [32], replicated, may hold values from 1 to 128, as said below
- range_filter: float32 [2, 65536], replicated, may hold values from -5 to 5
- azimuth_filters: float32 [2, 16, 4096], replicated, may hold values from -5 to 5
- set_index: int32 [65536], replicated, may hold values from 0 to 15, never falling along the last dimension, each value on 1 to 8192 neighbouring positions
Outputs:
- focused: bfloat16 [2, 4096, 65536], P(None, ('grp', 'line'))
Inputs may be any that keep to these rules, and one draw needn't show every extreme that they name: For every block b with b % (8) < 4, valid_lines[b] + valid_lines[b + 4] <= 160; in every draw one such pair holds exactly 128 and 32. `set_index`: never falls along the range.
All inputs are finite; a program needn't handle non-finite values.
Results may differ from a plain program's by a relative error of at most 0.014.
Values may be sent and summed in bfloat16 or wider, within the bound.
A program may use at most 320 MiB of HBM per device.

v0:
```python
import math

import jax
import jax.numpy as jnp
from jax import lax
from jax.sharding import PartitionSpec as P

RANGE = 65536
RANGE_LO = 256
AZ_INNER = 64
SETS = 16
RANGE_HI = 256


def fourier_table(length, sign_value):
    indices = jnp.arange(length, dtype=jnp.int32)
    phases = indices[:, None] * indices[None, :] % length
    angles = phases.astype(jnp.float32) * (2.0 * math.pi / length)
    cosine = jnp.cos(angles)
    sine_part = sign_value * jnp.sin(angles)
    top_rows = jnp.stack([cosine, -sine_part], axis=1)
    low_rows = jnp.stack([sine_part, cosine], axis=1)
    return jnp.stack([top_rows, low_rows], axis=0).astype(jnp.bfloat16)


def twiddle(row_len, col_len, total_len, sign_value):
    phases = (
        jnp.arange(row_len, dtype=jnp.int32)[:, None]
        * jnp.arange(col_len, dtype=jnp.int32)[None, :]
        % total_len
    )
    angles = phases.astype(jnp.float32) * (2.0 * math.pi / total_len)
    factor = 1.0 / math.sqrt(total_len)
    return (jnp.cos(angles) * factor, sign_value * jnp.sin(angles) * factor)


def rotate(values, cosine, sine_part):
    return jnp.stack(
        [cosine * values[0] - sine_part * values[1], sine_part * values[0] + cosine * values[1]],
        axis=0,
    )


def product(spec, left, right):
    return jnp.einsum(spec, left, right, preferred_element_type=jnp.float32)


def compress_lines(block, live_rows, range_filter):
    line_total = block.shape[1]
    high_len = RANGE_HI
    low_len = RANGE_LO
    grid_data = block.reshape(2, line_total, high_len, low_len)
    section_one = product("dkcn,clnb->dlkb", fourier_table(high_len, -1.0), grid_data)
    cosine, sine_part = twiddle(high_len, low_len, RANGE, -1.0)
    rotated = rotate(section_one, cosine, sine_part).astype(jnp.bfloat16)
    spectrum = product("dkcn,clan->dlak", fourier_table(low_len, -1.0), rotated)
    filter_grid = range_filter.reshape(2, low_len, high_len).transpose(0, 2, 1)
    shaped = jnp.stack(
        [
            spectrum[0] * filter_grid[0] - spectrum[1] * filter_grid[1],
            spectrum[0] * filter_grid[1] + spectrum[1] * filter_grid[0],
        ],
        axis=0,
    ).astype(jnp.bfloat16)
    back_section = product("dnck,clak->dlan", fourier_table(low_len, 1.0), shaped)
    cosine, sine_part = twiddle(high_len, low_len, RANGE, 1.0)
    turned = rotate(back_section, cosine, sine_part).astype(jnp.bfloat16)
    result = product("dnck,clkb->dlnb", fourier_table(high_len, 1.0), turned)
    result = result * live_rows[None, :, None, None]
    return result.astype(jnp.bfloat16).reshape(2, line_total, RANGE)


def focus_columns(columns, filter_grid):
    line_total = columns.shape[1]
    col_width = columns.shape[2]
    inner_len = AZ_INNER
    outer_len = line_total // inner_len
    grid_data = columns.reshape(2, outer_len, inner_len, col_width)
    section_one = product("dkcm,cmbx->dkbx", fourier_table(outer_len, -1.0), grid_data)
    cosine, sine_part = twiddle(outer_len, inner_len, line_total, -1.0)
    rotated = rotate(section_one, cosine[:, :, None], sine_part[:, :, None]).astype(jnp.bfloat16)
    spectrum = product("dkcm,camx->dakx", fourier_table(inner_len, -1.0), rotated)
    shaped = jnp.stack(
        [
            spectrum[0] * filter_grid[0] - spectrum[1] * filter_grid[1],
            spectrum[0] * filter_grid[1] + spectrum[1] * filter_grid[0],
        ],
        axis=0,
    ).astype(jnp.bfloat16)
    back_section = product("dmck,cakx->damx", fourier_table(inner_len, 1.0), shaped)
    cosine, sine_part = twiddle(outer_len, inner_len, line_total, 1.0)
    turned = rotate(back_section, cosine[:, :, None], sine_part[:, :, None]).astype(jnp.bfloat16)
    result = product("dmck,ckbx->dmbx", fourier_table(outer_len, 1.0), turned)
    return result.astype(jnp.bfloat16).reshape(2, line_total, col_width)


def per_device(raw_echo, valid_lines, range_filter, azimuth_filters, set_index):
    lines_here = raw_echo.shape[1]
    line_count = lax.axis_size("line")
    group_count = lax.axis_size("grp")
    group_id = lax.axis_index("grp")
    line_id = lax.axis_index("line")
    block_id = group_id * line_count + line_id
    own_valid = valid_lines[block_id]
    row_ids = jnp.arange(lines_here, dtype=jnp.int32)
    live_rows = (row_ids < own_valid).astype(jnp.float32)
    compressed = compress_lines(raw_echo, live_rows, range_filter)
    col_width = RANGE // (group_count * line_count)
    columns = lax.all_to_all(compressed, ("grp", "line"), split_axis=2, concat_axis=1, tiled=True)
    column_sets = lax.dynamic_slice_in_dim(set_index, block_id * col_width, col_width, 0)
    selector = (column_sets[:, None] == jnp.arange(SETS, dtype=jnp.int32)[None, :]).astype(
        jnp.float32
    )
    filter_table = azimuth_filters.reshape(2, SETS, AZ_INNER, -1).transpose(0, 1, 3, 2)
    chosen = jnp.einsum("dsab,xs->dabx", filter_table, selector, precision=lax.Precision.HIGHEST)
    focused_cols = focus_columns(columns, chosen)
    result = lax.all_to_all(focused_cols, ("grp", "line"), split_axis=1, concat_axis=2, tiled=True)
    return result


def solution(mesh):
    placed = (P(None, ("grp", "line"), None), P(), P(), P(), P())
    return jax.shard_map(
        per_device,
        mesh=mesh,
        in_specs=placed,
        out_specs=P(None, ("grp", "line"), None),
        check_vma=False,
    )
```

profile of v0, /device:TPU:0, one launch (start us, length us, event | category | flops | bytes accessed | tf_op | source)
XLA Modules:
  0.0 2477.1 jit_solution(9380637162662001340)
XLA Ops:
  0.0 1.0 negate_convert_fusion
  1.0 1.1 cosine_convert_fusion
  2.1 1.0 fusion.55
  3.1 1.1 cosine_multiply_fusion
  4.2 1.7 broadcast_multiply_fusion.1
  5.9 0.0 copy-start.2
  5.9 0.0 copy-start.8
  5.9 23.2 copy.110
  29.0 0.0 copy-done.2
  29.1 0.2 copy.66
  29.3 0.0 copy-done.8
  29.3 0.6 dynamic_slice.6
  29.9 1.2 compare_convert_fusion
  31.1 0.1 fusion.41
  31.2 44.6 %fusion.22 = f32[2,128,256,256]{3,2,1,0:T(8,128)} fusion(bf16[1,256,2,256]{3,1,2,0:T(8,128)(2,1)S(1)} %get-tuple-element.21, bf16[1,256,2,256]{3,1,2,0:T(8,128)(2,1)S(1)} %get-tuple-element.22, bf16[2,128,256,256]{3,2,1,0:T(8,128)(2,1)} %bitcast.173), kind=kOutput, calls=%fused_computation.45 | convolution fusion | flops 17180917760 | bytes 101187584 | tf_op jit(solution)/shard_map/dkcn,clnb->dlkb/dot_general | solution.py:45
  75.8 33.5 %subtract_convert_fusion.5 = (bf16[1,128,256,256]{3,2,1,0:T(8,128)(2,1)}, bf16[1,128,256,256]{3,2,1,0:T(8,128)(2,1)}) fusion(f32[2,128,256,256]{3,2,1,0:T(8,128)} %fusion.22, f32[256,256]{1,0:T(8,128)S(1)} %get-tuple-element.32, f32[256,256]{1,0:T(8,128)S(1)} %get-tuple-element.31), kind=kLoop, calls=%fused_computation.42 | loop fusion | flops 67108864 | bytes 101187584 | tf_op jit(solution)/shard_map/convert.18
  109.3 36.5 %fusion.25 = f32[2,128,256,256]{3,2,0,1:T(8,128)} fusion(bf16[1,256,2,256]{3,1,2,0:T(8,128)(2,1)S(1)} %get-tuple-element.21, bf16[1,256,2,256]{3,1,2,0:T(8,128)(2,1)S(1)} %get-tuple-element.22, bf16[1,128,256,256]{3,2,1,0:T(8,128)(2,1)} %get-tuple-element.12, bf16[1,128,256,256]{3,2,1,0:T(8,128)(2,1)} %get-tuple-element.11), kind=kOutput, calls=%fused_computation.46 | convolution fusion | flops 17197694976 | bytes 101187584 | tf_op jit(solution)/shard_map/dkcn,clan->dlak/dot_general | solution.py:45
  145.7 33.5 %subtract_convert_fusion.4 = (bf16[1,128,256,256]{3,2,0,1:T(8,128)(2,1)}, bf16[1,128,256,256]{3,2,0,1:T(8,128)(2,1)}) fusion(f32[2,128,256,256]{3,2,0,1:T(8,128)} %fusion.25, f32[256,256]{1,0:T(8,128)S(1)} %get-tuple-element.18, f32[256,256]{1,0:T(8,128)S(1)} %get-tuple-element.17), kind=kLoop, calls=%fused_computation.40 | loop fusion | flops 67108864 | bytes 101187584 | tf_op jit(solution)/shard_map/convert.16
  179.2 0.0 copy-start
  179.2 36.3 %fusion.31 = f32[2,128,256,256]{3,2,1,0:T(8,128)} fusion(bf16[1,128,256,256]{3,2,0,1:T(8,128)(2,1)} %get-tuple-element.10, bf16[1,128,256,256]{3,2,0,1:T(8,128)(2,1)} %get-tuple-element.9, bf16[1,256,2,256]{3,1,2,0:T(8,128)(2,1)S(1)} %get-tuple-element.20, bf16[1,256,2,256]{3,1,2,0:T(8,128)(2,1)S(1)} %get-tuple-element.19), kind=kOutput, calls=%fused_computation.48 | convolution fusion | flops 17248026624 | bytes 101187584 | tf_op jit(solution)/shard_map/dnck,clak->dlan/dot_general | solution.py:45
  215.5 0.0 copy-done
  215.5 0.0 copy-start.9
  215.5 33.4 %subtract_convert_fusion.3 = (bf16[1,128,256,256]{3,2,1,0:T(8,128)(2,1)}, bf16[1,128,256,256]{3,2,1,0:T(8,128)(2,1)}) fusion(f32[2,128,256,256]{3,2,1,0:T(8,128)} %fusion.31, f32[256,256]{1,0:T(8,128)S(1)} %copy-done, f32[256,256]{1,0:T(8,128)S(1)} %get-tuple-element.31), kind=kLoop, calls=%fused_computation.38 | loop fusion | flops 67108864 | bytes 101187584 | tf_op jit(solution)/shard_map/convert.6
  248.9 0.0 copy-done.9
  248.9 30.4 %fusion.1 = bf16[2,128,256,256]{2,3,0,1:T(8,128)(2,1)} fusion(f32[128]{0:T(128)S(1)} %copy-done.9, bf16[1,256,2,256]{3,1,2,0:T(8,128)(2,1)S(1)} %get-tuple-element.20, bf16[1,256,2,256]{3,1,2,0:T(8,128)(2,1)S(1)} %get-tuple-element.19, bf16[1,128,256,256]{3,2,1,0:T(8,128)(2,1)} %get-tuple-element.8, bf16[1,128,256,256]{3,2,1,0:T(8,128)(2,1)} %get-tuple-element.7), kind=kOutput, calls=%fused_computation.5 | convolution fusion | flops 17231249408 | bytes 67633664 | tf_op jit(solution)/shard_map/dnck,clkb->dlnb/dot_general | solution.py:45
  279.4 47.3 %copy.69 = bf16[2,128,256,256]{1,3,2,0:T(8,128)(2,1)} copy(bf16[2,128,256,256]{2,3,0,1:T(8,128)(2,1)} %fusion.1) | data formatting | bytes 67108864 | tf_op jit(solution)/shard_map/convert_element_type | solution.py:70
  326.7 60.1 %copy.70 = bf16[2,128,65536]{1,0,2:T(2,128)(2,1)} copy(bf16[2,128,65536]{1,2,0:T(8,128)(2,1)} %bitcast.167) | data formatting | bytes 67108864 | tf_op jit(solution)/shard_map/reshape | solution.py:70
  386.8 0.0 copy-start.1
  386.8 7.4 all-to-all-start
  394.2 0.0 copy-done.1
  394.2 0.4 reshape.311
  394.6 0.9 copy.96
  395.6 0.7 dynamic_slice.7
  396.3 0.1 fusion.82
  396.4 0.1 negate_convert_fusion.2
  396.6 0.1 cosine_convert_fusion.1
  396.7 0.8 broadcast_multiply_fusion.3
  397.5 0.2 cosine_multiply_fusion.1
  397.6 0.0 copy-start.3
  397.6 0.7 fusion.66
  398.3 31.1 %convolution_bitcast_fusion.1 = f32[2,64,64,2048]{3,2,0,1:T(8,128)} fusion(f32[2,16,64,64]{3,1,0,2:T(8,128)S(1)} %copy.96, s32[2048]{0:T(1024)S(1)} %dynamic_slice.7), kind=kOutput, calls=%fused_computation.43 | convolution fusion | flops 3221258240 | bytes 67641344 | tf_op jit(solution)/shard_map/dsab,xs->dabx/dot_general | solution.py:115
  429.4 689.0 %all-to-all-done = bf16[2,128,65536]{1,0,2:T(2,128)(2,1)} async-done(((bf16[2,128,65536]{1,0,2:T(2,128)(2,1)}), bf16[2,128,65536]{1,0,2:T(2,128)(2,1)}, u32[]{:S(2)}, u32[]{:S(2)}) %all-to-all-start) | async-done | bytes 33554464 | tf_op jit(solution)/shard_map/all_to_all | solution.py:109
  1118.4 23.0 copy.71
  1141.4 42.0 %copy.72 = bf16[2,32,128,2048]{3,2,1,0:T(8,128)(2,1)} copy(bf16[2,32,128,2048]{2,3,1,0:T(8,128)(2,1)} %bitcast.168) | data formatting | bytes 67108864 | tf_op jit(solution)/shard_map/all_to_all | solution.py:109
  1183.5 61.5 %convolution_bitcast_fusion = f32[2,64,64,2048]{3,1,2,0:T(8,128)} fusion(bf16[2,64,64,2048]{3,2,1,0:T(8,128)(2,1)} %bitcast.166, bf16[1,64,2,64]{3,1,2,0:T(8,128)(2,1)S(1)} %get-tuple-element.24, bf16[1,64,2,64]{3,1,2,0:T(8,128)(2,1)S(1)} %get-tuple-element.25), kind=kOutput, calls=%fused_computation.4 | convolution fusion | flops 4295032832 | bytes 100696064 | tf_op jit(solution)/shard_map/dkcm,cmbx->dkbx/dot_general | solution.py:45
  1245.0 0.0 copy-done.3
  1245.0 34.4 %subtract_convert_fusion.2 = (bf16[1,64,64,2048]{3,1,2,0:T(8,128)(2,1)}, bf16[1,64,64,2048]{3,1,2,0:T(8,128)(2,1)}) fusion(f32[2,64,64,2048]{3,1,2,0:T(8,128)} %convolution_bitcast_fusion, f32[64,64]{0,1:T(8,128)S(1)} %get-tuple-element.38, f32[64,64]{0,1:T(8,128)S(1)} %get-tuple-element.37), kind=kLoop, calls=%fused_computation.36 | loop fusion | flops 67108864 | bytes 100696064 | tf_op jit(solution)/shard_map/convert.4
  1279.4 23.0 maximum_bitcast_fusion.4
  1302.4 42.9 %fusion.28 = f32[2,64,64,2048]{3,2,0,1:T(8,128)} fusion(bf16[2,64,64,2048,1]{3,1,2,0,4:T(8,128)(2,1)} %maximum_bitcast_fusion.4, bf16[1,64,2,64]{3,1,2,0:T(8,128)(2,1)S(1)} %get-tuple-element.24, bf16[1,64,2,64]{3,1,2,0:T(8,128)(2,1)S(1)} %get-tuple-element.25), kind=kOutput, calls=%fused_computation.47 | convolution fusion | flops 4295032832 | bytes 100696064 | tf_op jit(solution)/shard_map/dkcm,camx->dakx/dot_general | solution.py:45
  1345.3 54.5 %subtract_convert_fusion.1 = (bf16[1,64,64,2048]{3,2,0,1:T(8,128)(2,1)}, bf16[1,64,64,2048]{3,2,0,1:T(8,128)(2,1)}) fusion(f32[2,64,64,2048]{3,2,0,1:T(8,128)} %convolution_bitcast_fusion.1, f32[2,64,64,2048]{3,2,0,1:T(8,128)} %fusion.28), kind=kLoop, calls=%fused_computation.34 | loop fusion | flops 67108864 | bytes 167772160 | tf_op jit(solution)/shard_map/convert.2
  1399.7 0.0 copy-done.6
  1399.8 0.0 copy-done.7
  1399.8 34.3 %fusion.21 = f32[64,2048,2,64]{1,3,2,0:T(8,128)} fusion(bf16[1,64,64,2048]{3,2,0,1:T(8,128)(2,1)} %get-tuple-element.6, bf16[1,64,64,2048]{3,2,0,1:T(8,128)(2,1)} %get-tuple-element.5, bf16[1,64,2,64]{3,1,2,0:T(8,128)(2,1)S(1)} %copy-done.7, bf16[1,64,2,64]{3,1,2,0:T(8,128)(2,1)S(1)} %copy-done.6), kind=kOutput, calls=%fused_computation.44 | convolution fusion | flops 4362141696 | bytes 100696064 | tf_op jit(solution)/shard_map/dmck,cakx->damx/dot_general | solution.py:45
  1434.0 56.4 %copy.143 = f32[64,2048,2,64]{1,0,3,2:T(8,128)} copy(f32[64,2048,2,64]{1,3,2,0:T(8,128)} %fusion.21) | data formatting | bytes 134217728 | tf_op jit(solution)/shard_map/dmck,cakx->damx/dot_general | solution.py:45
  1490.5 0.0 copy-done.4
  1490.5 0.0 copy-done.5
  1490.5 34.4 %subtract_convert_fusion = (bf16[1,64,64,2048]{3,1,2,0:T(8,128)(2,1)}, bf16[1,64,64,2048]{3,1,2,0:T(8,128)(2,1)}) fusion(f32[2,64,64,2048]{3,1,2,0:T(8,128)} %bitcast.161, f32[64,64]{0,1:T(8,128)S(1)} %copy-done.5, f32[64,64]{0,1:T(8,128)S(1)} %copy-done.4), kind=kLoop, calls=%fused_computation.32 | loop fusion | flops 67108864 | bytes 100696064 | tf_op jit(solution)/shard_map/convert
  1524.8 23.6 bitcast_convert_fusion
  1548.5 30.1 %copy.79 = bf16[2,64,64,2048]{3,2,1,0:T(8,128)(2,1)} copy(bf16[2,64,64,2048]{3,1,2,0:T(8,128)(2,1)} %bitcast_convert_fusion) | data formatting | bytes 67108864 | tf_op jit(solution)/shard_map/convert_element_type | solution.py:94
  1578.6 60.3 %copy.80 = bf16[2,4096,2048]{2,0,1:T(2,128)(2,1)} copy(bf16[2,4096,2048]{2,1,0:T(8,128)(2,1)} %bitcast.169) | data formatting | bytes 67108864 | tf_op jit(solution)/shard_map/reshape | solution.py:94
  1638.8 729.2 %all_to_all.33 = bf16[2,4096,2048]{2,0,1:T(2,128)(2,1)} all-to-all(bf16[2,4096,2048]{2,0,1:T(2,128)(2,1)} %copy.80), channel_id=1, replica_groups=mesh['grp'=4,'line'=8] {'grp','line'}, dimensions={1} | all-to-all | bytes 67108864 | tf_op jit(solution)/shard_map/all_to_all | solution.py:117
  2368.0 23.1 copy.81
  2391.2 41.8 %copy.82 = bf16[2,128,32,2048]{1,3,2,0:T(8,128)(2,1)} copy(bf16[2,128,32,2048]{3,1,2,0:T(8,128)(2,1)} %bitcast.170) | data formatting | bytes 67108864 | tf_op jit(solution)/shard_map/all_to_all | solution.py:117
  2433.0 44.0 %copy.83 = bf16[2,128,65536]{2,1,0:T(8,128)(2,1)} copy(bf16[2,128,65536]{1,2,0:T(8,128)(2,1)} %bitcast.171) | data formatting | bytes 67108864 | tf_op jit(solution)/shard_map/all_to_all | solution.py:117
  (6 shorter events, 0.1 us)
Async XLA Ops:
  5.9 23.2 copy-start.2
  5.9 23.5 copy-start.8
  179.2 36.3 %copy-start = (f32[256,256]{1,0:T(8,128)S(1)}, f32[256,256]{1,0:T(8,128)}, u32[]{:S(2)}) copy-start(f32[256,256]{1,0:T(8,128)} %broadcast_multiply_fusion.1) | copy-start | bytes 786436
  215.5 33.4 %copy-start.9 = (f32[128]{0:T(128)S(1)}, f32[128]{0:T(128)}, u32[]{:S(2)}) copy-start(f32[128]{0:T(128)} %compare_convert_fusion) | copy-start | bytes 1540
  386.8 7.4 copy-start.1
  386.8 731.6 %all-to-all-start = ((bf16[2,128,65536]{1,0,2:T(2,128)(2,1)}), bf16[2,128,65536]{1,0,2:T(2,128)(2,1)}, u32[]{:S(2)}, u32[]{:S(2)}) async-start(bf16[2,128,65536]{1,0,2:T(2,128)(2,1)} %copy.70), calls=%async_computation | async-start | bytes 67108864 | tf_op jit(solution)/shard_map/all_to_all | solution.py:109
  397.6 847.4 %copy-start.3 = (f32[64,64]{0,1:T(8,128)}, f32[64,64]{0,1:T(8,128)S(1)}, u32[]{:S(2)}) copy-start(f32[64,64]{0,1:T(8,128)S(1)} %get-tuple-element.37) | copy-start | bytes 49156
  1345.3 54.5 %copy-start.6 = (bf16[1,64,2,64]{3,1,2,0:T(8,128)(2,1)S(1)}, bf16[1,64,2,64]{3,1,2,0:T(8,128)(2,1)}, u32[]{:S(2)}) copy-start(bf16[1,64,2,64]{3,1,2,0:T(8,128)(2,1)} %get-tuple-element.23) | copy-start | bytes 49156
  1345.3 54.5 %copy-start.7 = (bf16[1,64,2,64]{3,1,2,0:T(8,128)(2,1)S(1)}, bf16[1,64,2,64]{3,1,2,0:T(8,128)(2,1)}, u32[]{:S(2)}) copy-start(bf16[1,64,2,64]{3,1,2,0:T(8,128)(2,1)} %get-tuple-element.26) | copy-start | bytes 49156
  1434.0 56.4 %copy-start.4 = (f32[64,64]{0,1:T(8,128)S(1)}, f32[64,64]{0,1:T(8,128)}, u32[]{:S(2)}) copy-start(f32[64,64]{0,1:T(8,128)} %copy-done.3) | copy-start | bytes 49156
  1434.0 56.5 %copy-start.5 = (f32[64,64]{0,1:T(8,128)S(1)}, f32[64,64]{0,1:T(8,128)}, u32[]{:S(2)}) copy-start(f32[64,64]{0,1:T(8,128)} %broadcast_multiply_fusion.3) | copy-start | bytes 49156
where the time goes:
time: 2490 us; the launch traced here: 2480 us
  blocking collectives  729 us (29%)
  waiting for transfers between devices  689 us (28%)
  local copies, waits for them, and re-layouts  454 us (18%)
  matrix products  341 us (14%)
  other arithmetic  256 us (10%)
    all_to_all x1, blocking collectives, per_device(): lax.all_to_all(focused_cols, ('grp', 'line'), split_axis=1, concat_axis=2...  729 us
    all_to_all x1, waiting for transfers between devices, per_device(): lax.all_to_all(compressed, ('grp', 'line'), split_axis=2, concat_axis=1,...  689 us
    dot_general x8, matrix products, product(): return jnp.einsum(spec, left, right, preferred_element_type=jnp.float32)  310 us
    another operation x12, other arithmetic  227 us
    all_to_all x3, local copies, waits for them, and re-layouts, per_device(): lax.all_to_all(focused_cols, ('grp', 'line'), split_axis=1, concat_axis=2...  109 us
    all_to_all x2, local copies, waits for them, and re-layouts, per_device(): lax.all_to_all(compressed, ('grp', 'line'), split_axis=2, concat_axis=1,...  65.1 us
    reshape x1, local copies, waits for them, and re-layouts, focus_columns(): return result.astype(jnp.bfloat16).reshape(2, line_total, col_width)  60.3 us
    reshape x1, local copies, waits for them, and re-layouts, compress_lines(): return result.astype(jnp.bfloat16).reshape(2, line_total, RANGE)  60.1 us
  transfers between devices with their start and end apart: 1, of which 1 were waited for; matrix products, arithmetic and copies ran while one was open for 1% of the time, Pallas kernels for 0%

commit v1 on v0

v1 whole, which is shorter than its diff:
```python
import functools
import math

import jax
import jax.numpy as jnp
from jax import lax
from jax.experimental import pallas as pl
from jax.experimental.pallas import tpu as pltpu
from jax.sharding import PartitionSpec as P

RANGE_LO = 256
AZ_INNER = 64
GROUP = 16
LANES = 128
CHUNK = 256
SLOTS = 4
STRIDE = 5


def fourier(length, sign_value):
    indices = jnp.arange(length, dtype=jnp.int32)
    phases = indices[:, None] * indices[None, :] % length
    angles = phases.astype(jnp.float32) * (2.0 * math.pi / length)
    return jnp.cos(angles), sign_value * jnp.sin(angles)


def left_table(length, sign_value):
    c, s = fourier(length, sign_value)
    return jnp.concatenate(
        [jnp.concatenate([c, -s], 1), jnp.concatenate([s, c], 1)], 0
    ).astype(jnp.bfloat16)


def right_table(length, sign_value):
    c, s = fourier(length, sign_value)
    return jnp.concatenate(
        [jnp.concatenate([c, s], 1), jnp.concatenate([-s, c], 1)], 0
    ).astype(jnp.bfloat16)


def twiddle(row_len, col_len, total_len):
    phases = (
        jnp.arange(row_len, dtype=jnp.int32)[:, None]
        * jnp.arange(col_len, dtype=jnp.int32)[None, :]
        % total_len
    )
    angles = phases.astype(jnp.float32) * (2.0 * math.pi / total_len)
    factor = 1.0 / math.sqrt(total_len)
    return jnp.stack([jnp.cos(angles) * factor, jnp.sin(angles) * factor])


def mul(m, x):
    return jnp.dot(m, x, preferred_element_type=jnp.float32)


def range_lines(first, live_ref, etab, vtab, ftab, xs, hi, lo):
    halves = lo // LANES

    def line(j, carry):
        def take(c):
            parts = [
                xs[c, h, pl.ds(j, hi, stride=GROUP), :].astype(jnp.bfloat16)
                for h in range(halves)
            ]
            return jnp.concatenate(parts, 1)

        x = jnp.concatenate([take(0), take(1)], 0)
        s = mul(etab[0], x)
        sr, si = s[:hi], s[hi:]
        vr, vi = vtab[0], vtab[1]
        q = jnp.concatenate(
            [
                (vr * sr + vi * si).astype(jnp.bfloat16),
                (vr * si - vi * sr).astype(jnp.bfloat16),
            ],
            1,
        )
        s = mul(q, etab[1])
        sr, si = s[:, :lo], s[:, lo:]
        fr, fi = ftab[0], ftab[1]
        q = jnp.concatenate(
            [
                (sr * fr - si * fi).astype(jnp.bfloat16),
                (sr * fi + si * fr).astype(jnp.bfloat16),
            ],
            1,
        )
        s = mul(q, etab[2])
        sr, si = s[:, :lo], s[:, lo:]
        z = jnp.concatenate(
            [
                (vr * sr - vi * si).astype(jnp.bfloat16),
                (vi * sr + vr * si).astype(jnp.bfloat16),
            ],
            0,
        )
        s = mul(etab[3], z) * live_ref[first + j]
        for h in range(halves):
            cols = slice(h * LANES, (h + 1) * LANES)
            xs[0, h, pl.ds(j, hi, stride=GROUP), :] = s[:hi, cols]
            xs[1, h, pl.ds(j, hi, stride=GROUP), :] = s[hi:, cols]
        return carry

    lax.fori_loop(0, GROUP, line, 0, unroll=2)


def place(devices):
    line_count = lax.axis_size("line")
    me = lax.axis_index("grp") * line_count + lax.axis_index("line")

    def peer(step):
        d = lax.rem(me + step * STRIDE, devices)
        return d, (lax.div(d, line_count), lax.rem(d, line_count))

    return me, peer


def greet(devices, peer):
    barrier = pltpu.get_barrier_semaphore()

    def signal(step, carry):
        pl.semaphore_signal(
            barrier, inc=1, device_id=peer(step)[1], device_id_type=pl.DeviceIdType.MESH
        )
        return carry

    lax.fori_loop(1, devices, signal, 0)
    pl.semaphore_wait(barrier, devices - 1)


def range_kernel(
    devices, live_ref, raw, etab, vtab, ftab, recv, xbuf, xs, stage, x_sem, own_sem, send_sem, recv_sem
):
    _, lines, cols = raw.shape
    width = recv.shape[-1]
    lo = vtab.shape[-1]
    hi = cols // lo
    halves = lo // LANES
    groups = lines // GROUP
    me, peer = place(devices)

    def fetch(g):
        rows = pl.ds(pl.multiple_of(g * GROUP, GROUP), GROUP)
        slot = lax.rem(g, 2)
        return pltpu.make_async_copy(raw.at[:, rows, :], xbuf.at[slot], x_sem.at[slot])

    def own_copy(g):
        rows = pl.ds(pl.multiple_of(g * GROUP, GROUP), GROUP)
        slot = lax.rem(g, SLOTS)
        mine = pl.ds(pl.multiple_of(me * width, width), width)
        return pltpu.make_async_copy(
            stage.at[slot, :, :, mine], recv.at[me, :, rows, :], own_sem.at[slot]
        )

    def drain(g):
        slot = lax.rem(g, SLOTS)
        own_copy(g).wait()
        sent = stage.at[slot, :, :, pl.ds(0, (devices - 1) * width)]
        pltpu.make_async_copy(sent, sent, send_sem.at[slot]).wait()

    fetch(0).start()
    greet(devices, peer)

    def group(g, carry):
        slot, now = lax.rem(g, SLOTS), lax.rem(g, 2)

        @pl.when(g + 1 < groups)
        def _():
            fetch(g + 1).start()

        fetch(g).wait()

        def load(n, carry):
            for c in range(2):
                for h in range(halves):
                    col = pl.multiple_of(n * lo + h * LANES, LANES)
                    row = pl.multiple_of(n * GROUP, GROUP)
                    xs[c, h, pl.ds(row, GROUP), :] = xbuf[now, c, :, pl.ds(col, LANES)].astype(
                        jnp.float32
                    )
            return carry

        lax.fori_loop(0, hi, load, 0, unroll=4)
        range_lines(g * GROUP, live_ref, etab, vtab, ftab, xs, hi, lo)

        @pl.when(g >= SLOTS)
        def _():
            drain(g - SLOTS)

        def save(n, carry):
            for c in range(2):
                for h in range(halves):
                    col = pl.multiple_of(n * lo + h * LANES, LANES)
                    row = pl.multiple_of(n * GROUP, GROUP)
                    stage[slot, c, :, pl.ds(col, LANES)] = xs[c, h, pl.ds(row, GROUP), :].astype(
                        jnp.bfloat16
                    )
            return carry

        lax.fori_loop(0, hi, save, 0, unroll=4)
        own_copy(g).start()

        def send(step, carry):
            d, target = peer(step)
            rows = pl.ds(pl.multiple_of(g * GROUP, GROUP), GROUP)
            pltpu.make_async_remote_copy(
                src_ref=stage.at[slot, :, :, pl.ds(pl.multiple_of(d * width, width), width)],
                dst_ref=recv.at[me, :, rows, :],
                send_sem=send_sem.at[slot],
                recv_sem=recv_sem.at[0],
                device_id=target,
                device_id_type=pl.DeviceIdType.MESH,
            ).start()
            return carry

        lax.fori_loop(1, devices, send, 0)
        return carry

    lax.fori_loop(0, groups, group, 0)
    for g in range(max(0, groups - SLOTS), groups):
        drain(jnp.int32(g))
    arrived = recv.at[pl.ds(0, devices - 1)]
    pltpu.make_async_copy(arrived, arrived, recv_sem.at[0]).wait()


def compress(raw, live, etab, vtab, ftab, devices):
    _, lines, cols = raw.shape
    lo = RANGE_LO
    hi = cols // lo
    vmem = pl.BlockSpec(memory_space=pltpu.VMEM)
    hbm = pl.BlockSpec(memory_space=pl.ANY)
    return pl.pallas_call(
        functools.partial(range_kernel, devices),
        out_shape=jax.ShapeDtypeStruct((devices, 2, lines, cols // devices), jnp.bfloat16),
        in_specs=[pl.BlockSpec(memory_space=pltpu.SMEM), hbm, vmem, vmem, vmem],
        out_specs=hbm,
        scratch_shapes=[
            pltpu.VMEM((2, 2, GROUP, cols), jnp.bfloat16),
            pltpu.VMEM((2, lo // LANES, hi * GROUP, LANES), jnp.float32),
            pltpu.VMEM((SLOTS, 2, GROUP, cols), jnp.bfloat16),
            pltpu.SemaphoreType.DMA((2,)),
            pltpu.SemaphoreType.DMA((SLOTS,)),
            pltpu.SemaphoreType.DMA((SLOTS,)),
            pltpu.SemaphoreType.DMA((1,)),
        ],
        compiler_params=pltpu.CompilerParams(
            vmem_limit_bytes=56 << 20, collective_id=0, has_side_effects=True
        ),
        name="range_compress",
    )(live, raw, etab, vtab, ftab)


def azimuth_columns(etab, ttab, filt, pick, us, outer, inner):
    halves = CHUNK // LANES

    def take(rows):
        return jnp.concatenate(
            [
                jnp.concatenate(
                    [us[c, h, rows, :].astype(jnp.bfloat16) for h in range(halves)], 1
                )
                for c in range(2)
            ],
            0,
        )

    def put(rows, h, re, im):
        us[0, h, rows, :] = re
        us[1, h, rows, :] = im

    def first(m, carry):
        rows = pl.ds(m, outer, stride=inner)
        s = mul(etab[0], take(rows))
        vr, vi = ttab[0, m], ttab[1, m]
        for h in range(halves):
            cols = slice(h * LANES, (h + 1) * LANES)
            sr, si = s[:outer, cols], s[outer:, cols]
            put(rows, h, vr * sr + vi * si, vr * si - vi * sr)
        return carry

    def second(k, carry):
        rows = pl.ds(pl.multiple_of(k * inner, inner), inner)
        s = mul(etab[0], take(rows))
        f = mul(filt[k], pick)
        sr, si = s[:inner], s[inner:]
        fr, fi = f[:inner], f[inner:]
        b = jnp.concatenate(
            [
                (sr * fr - si * fi).astype(jnp.bfloat16),
                (sr * fi + si * fr).astype(jnp.bfloat16),
            ],
            0,
        )
        s = mul(etab[1], b)
        vr, vi = ttab[0, k], ttab[1, k]
        for h in range(halves):
            cols = slice(h * LANES, (h + 1) * LANES)
            sr, si = s[:inner, cols], s[inner:, cols]
            put(rows, h, vr * sr - vi * si, vi * sr + vr * si)
        return carry

    def last(m, carry):
        rows = pl.ds(m, outer, stride=inner)
        s = mul(etab[1], take(rows))
        for h in range(halves):
            cols = slice(h * LANES, (h + 1) * LANES)
            put(rows, h, s[:outer, cols], s[outer:, cols])
        return carry

    lax.fori_loop(0, inner, first, 0, unroll=4)
    lax.fori_loop(0, outer, second, 0, unroll=4)
    lax.fori_loop(0, inner, last, 0, unroll=4)


def pick_rows(sets_row, sets):
    row = lax.broadcasted_iota(jnp.int32, (3 * sets, CHUNK), 0) % sets
    return jnp.where(row == sets_row, 1.0, 0.0).astype(jnp.bfloat16)


def azimuth_kernel(
    devices, sets, s_ref, columns, etab, ttab, filt, out, ubuf, us, stage, u_sem, own_sem, send_sem, recv_sem
):
    _, _, lines, width = columns.shape
    inner = AZ_INNER
    outer = devices * lines // inner
    halves = CHUNK // LANES
    chunks = width // CHUNK
    me, peer = place(devices)

    def fetch(j):
        cols = pl.ds(pl.multiple_of(j * CHUNK, CHUNK), CHUNK)
        slot = lax.rem(j, 2)
        return pltpu.make_async_copy(columns.at[:, :, :, cols], ubuf.at[slot], u_sem.at[slot])

    def home(j):
        return out.at[:, :, pl.ds(pl.multiple_of(me * width + j * CHUNK, CHUNK), CHUNK)]

    def own_copy(j):
        slot = lax.rem(j, SLOTS)
        return pltpu.make_async_copy(stage.at[slot, me], home(j), own_sem.at[slot])

    def drain(j):
        slot = lax.rem(j, SLOTS)
        own_copy(j).wait()
        sent = stage.at[slot, pl.ds(0, devices - 1)]
        pltpu.make_async_copy(sent, sent, send_sem.at[slot]).wait()

    fetch(0).start()
    greet(devices, peer)

    def chunk(j, carry):
        slot, now = lax.rem(j, SLOTS), lax.rem(j, 2)

        @pl.when(j + 1 < chunks)
        def _():
            fetch(j + 1).start()

        fetch(j).wait()

        def load(b, carry):
            for c in range(2):
                for h in range(halves):
                    row = pl.multiple_of(b * lines, lines)
                    us[c, h, pl.ds(row, lines), :] = ubuf[
                        now, b, c, :, h * LANES : (h + 1) * LANES
                    ].astype(jnp.float32)
            return carry

        lax.fori_loop(0, devices, load, 0)
        pick = pick_rows(s_ref[j], sets)
        azimuth_columns(etab, ttab, filt, pick, us, outer, inner)

        @pl.when(j >= SLOTS)
        def _():
            drain(j - SLOTS)

        def save(b, carry):
            for c in range(2):
                for h in range(halves):
                    row = pl.multiple_of(b * lines, lines)
                    stage[slot, b, c, :, h * LANES : (h + 1) * LANES] = us[
                        c, h, pl.ds(row, lines), :
                    ].astype(jnp.bfloat16)
            return carry

        lax.fori_loop(0, devices, save, 0)
        own_copy(j).start()

        def send(step, carry):
            d, target = peer(step)
            pltpu.make_async_remote_copy(
                src_ref=stage.at[slot, d],
                dst_ref=home(j),
                send_sem=send_sem.at[slot],
                recv_sem=recv_sem.at[0],
                device_id=target,
                device_id_type=pl.DeviceIdType.MESH,
            ).start()
            return carry

        lax.fori_loop(1, devices, send, 0)
        return carry

    lax.fori_loop(0, chunks, chunk, 0)
    for j in range(max(0, chunks - SLOTS), chunks):
        drain(jnp.int32(j))
    arrived = out.at[:, :, pl.ds(0, (devices - 1) * width)]
    pltpu.make_async_copy(arrived, arrived, recv_sem.at[0]).wait()


def focus(columns, column_sets, etab, ttab, filt, sets):
    devices, _, lines, width = columns.shape
    vmem = pl.BlockSpec(memory_space=pltpu.VMEM)
    hbm = pl.BlockSpec(memory_space=pl.ANY)
    return pl.pallas_call(
        functools.partial(azimuth_kernel, devices, sets),
        out_shape=jax.ShapeDtypeStruct((2, lines, devices * width), jnp.bfloat16),
        in_specs=[vmem, hbm, vmem, vmem, vmem],
        out_specs=hbm,
        scratch_shapes=[
            pltpu.VMEM((2, devices, 2, lines, CHUNK), jnp.bfloat16),
            pltpu.VMEM((2, CHUNK // LANES, devices * lines, LANES), jnp.float32),
            pltpu.VMEM((SLOTS, devices, 2, lines, CHUNK), jnp.bfloat16),
            pltpu.SemaphoreType.DMA((2,)),
            pltpu.SemaphoreType.DMA((SLOTS,)),
            pltpu.SemaphoreType.DMA((SLOTS,)),
            pltpu.SemaphoreType.DMA((1,)),
        ],
        compiler_params=pltpu.CompilerParams(
            vmem_limit_bytes=56 << 20, collective_id=1, has_side_effects=True
        ),
        name="azimuth_focus",
    )(column_sets, columns, etab, ttab, filt)


def per_device(raw_echo, valid_lines, range_filter, azimuth_filters, set_index):
    _, lines, cols = raw_echo.shape
    line_count = lax.axis_size("line")
    devices = lax.axis_size("grp") * line_count
    block_id = lax.axis_index("grp") * line_count + lax.axis_index("line")
    lo = RANGE_LO
    hi = cols // lo
    width = cols // devices
    inner = AZ_INNER
    outer = devices * lines // inner
    assert hi == lo and outer == inner

    live = (jnp.arange(lines, dtype=jnp.int32) < valid_lines[block_id]).astype(jnp.float32)
    etab = jnp.stack(
        [left_table(hi, -1.0), right_table(lo, -1.0), right_table(lo, 1.0), left_table(hi, 1.0)]
    )
    vtab = twiddle(hi, lo, cols)
    ftab = range_filter.reshape(2, lo, hi).transpose(0, 2, 1)
    columns = compress(raw_echo, live, etab, vtab, ftab, devices)

    sets = azimuth_filters.shape[1]
    aztab = jnp.stack([left_table(inner, -1.0), left_table(inner, 1.0)])
    ttab = jnp.broadcast_to(
        twiddle(inner, outer, inner * outer)[..., None], (2, inner, outer, LANES)
    )
    filt = azimuth_filters.reshape(2, sets, inner, outer).transpose(3, 0, 2, 1)
    filt = filt.reshape(outer, 2 * inner, sets)
    high = lax.reduce_precision(filt, 8, 7)
    mid = lax.reduce_precision(filt - high, 8, 7)
    low = filt - high - mid
    filt = jnp.concatenate([high, mid, low], -1).astype(jnp.bfloat16)
    column_sets = lax.dynamic_slice_in_dim(set_index, block_id * width, width, 0)
    column_sets = column_sets.reshape(width // CHUNK, 1, CHUNK)
    return focus(columns, column_sets, aztab, ttab, filt, sets)


def solution(mesh):
    placed = (P(None, ("grp", "line"), None), P(), P(), P(), P())
    return jax.shard_map(
        per_device,
        mesh=mesh,
        in_specs=placed,
        out_specs=P(None, ("grp", "line"), None),
        check_vma=False,
    )
```

time: 2490 us -> 1580 us (0.63)
  Pallas kernels: 0 us -> 1530 us
  blocking collectives: 729 us -> 0 us
  waiting for transfers between devices: 689 us -> 0 us
  local copies, waits for them, and re-layouts: 454 us -> 34.1 us
  matrix products: 341 us -> 0 us
  other arithmetic: 256 us -> 9.34 us
    pallas_call x0 -> x2, Pallas kernels: none -> 1530 us  [the longest x1 775 us: focus(): pl.pallas_call(functools.partial(azimuth_kernel, devices, sets), out_shap...]
    all_to_all x1 -> x0, blocking collectives: 729 us -> none  [per_device(): lax.all_to_all(focused_cols, ('grp', 'line'), split_axis=1, concat_axis=2...]
    all_to_all x1 -> x0, waiting for transfers between devices: 689 us -> none  [per_device(): lax.all_to_all(compressed, ('grp', 'line'), split_axis=2, concat_axis=1,...]
    dot_general x9 -> x0, matrix products: 341 us -> none  [the longest x8 310 us: product(): return jnp.einsum(spec, left, right, preferred_element_type=jnp.float32)]
    another operation x15 -> x11, other arithmetic: 251 us -> 6.59 us
    all_to_all x5 -> x0, local copies, waits for them, and re-layouts: 174 us -> none  [the longest x3 109 us: per_device(): lax.all_to_all(focused_cols, ('grp', 'line'), split_axis=1, concat_axis=2...]
    reshape x4, local copies, waits for them, and re-layouts: 121 us -> 3.17 us  [the longest x2 1.62 us: per_device(): filt = azimuth_filters.reshape(2, sets, inner, outer).transpose(3, 0, 2, 1)]
    convert_element_type x2 -> x0, local copies, waits for them, and re-layouts: 77.4 us -> none  [the longest x1 47.3 us: compress_lines(): return result.astype(jnp.bfloat16).reshape(2, line_total, RANGE)]
  transfers between devices with their start and end apart: 1 -> 0, of which waited for: 1 -> 0; matrix products, arithmetic and copies ran while one was open for 1% -> 0% of each run, Pallas kernels for 0% -> 0%
where the time goes in v1:
time: 1580 us; the launch traced here: 1570 us
  Pallas kernels  1530 us (97%)
  local copies, waits for them, and re-layouts  34.1 us (2%)
    pallas_call x1, Pallas kernels, focus(): pl.pallas_call(functools.partial(azimuth_kernel, devices, sets), out_shap...  775 us
    pallas_call x1, Pallas kernels, compress(): pl.pallas_call(functools.partial(range_kernel, devices), out_shape=jax.Sh...  757 us

profile of v1, /device:TPU:0, one launch (start us, length us, event | category | flops | bytes accessed | tf_op | source)
XLA Modules:
  0.0 1574.8 jit_solution(8037805641929587278)
XLA Ops:
  0.0 0.0 copy-start
  0.0 1.3 dynamic_slice.7
  1.3 1.2 compare_convert_fusion.live_ref
  2.5 1.3 dynamic_slice.6
  3.8 0.1 fusion.36
  4.0 0.1 cosine_convert_fusion.1
  4.1 0.1 negate_convert_fusion.2
  4.3 0.1 maximum_bitcast_fusion
  4.4 0.6 maximum_maximum_fusion.1.etab
  5.0 0.2 sine_multiply_fusion.1
  5.2 1.0 fusion.22
  6.1 1.1 cosine_convert_fusion
  7.3 1.0 negate_convert_fusion
  8.3 1.1 copy.14
  9.3 1.0 copy.9
  10.3 1.1 sine_multiply_fusion
  11.4 0.8 pad_maximum_fusion.1.vtab
  12.2 0.0 copy-done
  12.2 0.4 reshape.349
  12.6 1.2 copy.10
  13.9 0.6 reshape.350
  14.4 0.1 reduce-precision_convert_fusion.1
  14.6 0.1 pad_maximum_fusion
  14.6 1.8 copy.11.filt
  16.4 0.2 fusion.5
  16.6 1.4 maximum_maximum_fusion.etab
  18.1 2.6 broadcast_in_dim.2.ttab
  20.7 756.5 %range_compress.1.columns = bf16[32,2,128,2048]{3,2,1,0:T(8,128)(2,1)} custom-call(f32[128]{0:T(128)} %compare_convert_fusion.live_ref, bf16[2,128,65536]{2,1,0:T(8,128)(2,1)} %raw.1, bf16[4,512,512]{2,1,0:T(8,128)(2,1)} %maximum_maximum_fusion.etab, f32[2,256,256]{2,1,0:T(8,128)} %pad_maximum_fusion.1.vtab, f32[2,256,256]{2,1,0:T(8,128)} %bitcast.35), custom_call_target="tpu_custom_call" | custom-call | tf_op jit(solution)/shard_map/range_compress/pallas_call | solution.py:232
  777.2 774.7 %azimuth_focus.1 = bf16[2,128,65536]{2,1,0:T(8,128)(2,1)} custom-call(s32[8,1,256]{2,1,0:T(1,128)} %bitcast.38, bf16[32,2,128,2048]{3,2,1,0:T(8,128)(2,1)} %range_compress.1.columns, bf16[2,128,128]{2,1,0:T(8,128)(2,1)} %maximum_maximum_fusion.1.etab, f32[2,64,64,128]{3,2,1,0:T(8,128)} %broadcast_in_dim.2.ttab, bf16[64,128,48]{2,1,0:T(8,128)(2,1)} %copy.11.filt), custom_call_target="tpu_custom_call" | custom-call | tf_op jit(solution)/shard_map/azimuth_focus/pallas_call | solution.py:415
  1551.9 22.9 %copy.16 = bf16[2,128,65536]{2,1,0:T(8,128)(2,1)} copy(bf16[2,128,65536]{2,1,0:T(8,128)(2,1)} %azimuth_focus.1) | data formatting | bytes 67108864
  (1 shorter events, 0.0 us)
Async XLA Ops:
  0.0 12.2 copy-start

commit v2 on v1

--- a/solution.py
+++ b/solution.py
@@ -3,6 +3,7 @@
 
 import jax
 import jax.numpy as jnp
+import numpy as np
 from jax import lax
 from jax.experimental import pallas as pl
 from jax.experimental.pallas import tpu as pltpu
@@ -18,35 +19,35 @@
 
 
 def fourier(length, sign_value):
-    indices = jnp.arange(length, dtype=jnp.int32)
+    indices = np.arange(length, dtype=np.int64)
     phases = indices[:, None] * indices[None, :] % length
-    angles = phases.astype(jnp.float32) * (2.0 * math.pi / length)
-    return jnp.cos(angles), sign_value * jnp.sin(angles)
+    angles = phases.astype(np.float32) * (2.0 * math.pi / length)
+    return np.cos(angles), sign_value * np.sin(angles)
 
 
 def left_table(length, sign_value):
     c, s = fourier(length, sign_value)
-    return jnp.concatenate(
-        [jnp.concatenate([c, -s], 1), jnp.concatenate([s, c], 1)], 0
-    ).astype(jnp.bfloat16)
+    return np.concatenate(
+        [np.concatenate([c, -s], 1), np.concatenate([s, c], 1)], 0
+    )
 
 
 def right_table(length, sign_value):
     c, s = fourier(length, sign_value)
-    return jnp.concatenate(
-        [jnp.concatenate([c, s], 1), jnp.concatenate([-s, c], 1)], 0
-    ).astype(jnp.bfloat16)
+    return np.concatenate(
+        [np.concatenate([c, s], 1), np.concatenate([-s, c], 1)], 0
+    )
 
 
 def twiddle(row_len, col_len, total_len):
     phases = (
-        jnp.arange(row_len, dtype=jnp.int32)[:, None]
-        * jnp.arange(col_len, dtype=jnp.int32)[None, :]
+        np.arange(row_len, dtype=np.int64)[:, None]
+        * np.arange(col_len, dtype=np.int64)[None, :]
         % total_len
     )
-    angles = phases.astype(jnp.float32) * (2.0 * math.pi / total_len)
+    angles = phases.astype(np.float32) * (2.0 * math.pi / total_len)
     factor = 1.0 / math.sqrt(total_len)
-    return jnp.stack([jnp.cos(angles) * factor, jnp.sin(angles) * factor])
+    return np.stack([np.cos(angles) * factor, np.sin(angles) * factor]).astype(np.float32)
 
 
 def mul(m, x):
@@ -446,17 +447,18 @@
     assert hi == lo and outer == inner
 
     live = (jnp.arange(lines, dtype=jnp.int32) < valid_lines[block_id]).astype(jnp.float32)
-    etab = jnp.stack(
+    etab = np.stack(
         [left_table(hi, -1.0), right_table(lo, -1.0), right_table(lo, 1.0), left_table(hi, 1.0)]
-    )
-    vtab = twiddle(hi, lo, cols)
+    ).astype(jnp.bfloat16)
+    etab, vtab = jnp.asarray(etab), jnp.asarray(twiddle(hi, lo, cols))
     ftab = range_filter.reshape(2, lo, hi).transpose(0, 2, 1)
     columns = compress(raw_echo, live, etab, vtab, ftab, devices)
 
     sets = azimuth_filters.shape[1]
-    aztab = jnp.stack([left_table(inner, -1.0), left_table(inner, 1.0)])
+    aztab = np.stack([left_table(inner, -1.0), left_table(inner, 1.0)])
+    aztab = jnp.asarray(aztab.astype(jnp.bfloat16))
     ttab = jnp.broadcast_to(
-        twiddle(inner, outer, inner * outer)[..., None], (2, inner, outer, LANES)
+        jnp.asarray(twiddle(inner, outer, inner * outer))[..., None], (2, inner, outer, LANES)
     )
     filt = azimuth_filters.reshape(2, sets, inner, outer).transpose(3, 0, 2, 1)
     filt = filt.reshape(outer, 2 * inner, sets)

time: 1580 us -> 1570 us (level)
  no operation moved by 1% of the time
where the time goes in v2:
time: 1570 us
  Pallas kernels  1530 us (97%)
  local copies, waits for them, and re-layouts  34.1 us (2%)
    pallas_call x1, Pallas kernels, focus(): pl.pallas_call(functools.partial(azimuth_kernel, devices, sets), out_shap...  776 us
    pallas_call x1, Pallas kernels, compress(): pl.pallas_call(functools.partial(range_kernel, devices), out_shape=jax.Sh...  757 us

profile of v2, /device:TPU:0, one launch (start us, length us, event | category | flops | bytes accessed | tf_op | source)
XLA Modules:
  0.0 1568.4 jit_solution(18252048902886804517)
XLA Ops:
  0.0 0.0 copy-start
  0.0 1.3 dynamic_slice.7
  1.3 1.2 compare_convert_fusion.live_ref
  2.5 1.3 dynamic_slice.6
  3.8 1.1 copy.18
  4.9 1.0 copy.13
  5.9 0.0 copy-done
  5.9 0.4 reshape.15
  6.3 1.2 copy.14
  7.5 0.6 reshape.16
  8.1 0.1 reduce-precision_convert_fusion.1
  8.3 0.1 pad_maximum_fusion
  8.3 1.8 copy.15.filt
  10.1 0.0 copy-start.1
  10.1 756.6 %range_compress.1.columns = bf16[32,2,128,2048]{3,2,1,0:T(8,128)(2,1)} custom-call(f32[128]{0:T(128)} %compare_convert_fusion.live_ref, bf16[2,128,65536]{2,1,0:T(8,128)(2,1)} %raw.1, bf16[4,512,512]{2,1,0:T(8,128)(2,1)} %constant.26.clone.etab, f32[2,256,256]{2,1,0:T(8,128)} %constant.27.clone.vtab, f32[2,256,256]{2,1,0:T(8,128)} %bitcast.11), custom_call_target="tpu_custom_call" | custom-call | tf_op jit(solution)/shard_map/range_compress/pallas_call | solution.py:233
  766.7 0.0 copy-done.1
  766.7 2.6 broadcast_in_dim.2.ttab
  769.3 776.2 %azimuth_focus.1 = bf16[2,128,65536]{2,1,0:T(8,128)(2,1)} custom-call(s32[8,1,256]{2,1,0:T(1,128)} %bitcast.14, bf16[32,2,128,2048]{3,2,1,0:T(8,128)(2,1)} %range_compress.1.columns, bf16[2,128,128]{2,1,0:T(8,128)(2,1)} %constant.28.clone.etab, f32[2,64,64,128]{3,2,1,0:T(8,128)} %broadcast_in_dim.2.ttab, bf16[64,128,48]{2,1,0:T(8,128)(2,1)} %copy.15.filt), custom_call_target="tpu_custom_call" | custom-call | tf_op jit(solution)/shard_map/azimuth_focus/pallas_call | solution.py:416
  1545.6 22.9 %copy.20 = bf16[2,128,65536]{2,1,0:T(8,128)(2,1)} copy(bf16[2,128,65536]{2,1,0:T(8,128)(2,1)} %azimuth_focus.1) | data formatting | bytes 67108864
Async XLA Ops:
  0.0 5.9 copy-start
  10.1 756.6 %copy-start.1 = (f32[2,64,64]{2,1,0:T(8,128)S(1)}, f32[2,64,64]{2,1,0:T(8,128)}, u32[]{:S(2)}) copy-start(f32[2,64,64]{2,1,0:T(8,128)} %constant.29.clone) | copy-start | bytes 98308
